TPU v7x, 32 devices: a whole 2x2x4 slice. The times are simulated.
32 devices in a mesh: groups: 2 (over x), freq: 16 (over z, y, core).
Axes of the slice: x: 2, y: 2, z: 4, core: 2. Of those that a mesh axis runs over, the one named last changes fastest.
Arguments:
- voltages: bfloat16 [32, 263, 2, 2, 2048], P(('groups', 'freq')), parts along dimension 0, may hold values from -12 to 12
- pfb_taps: float32 [8, 2], replicated, may hold values from 0.2 to 1
- steering: bfloat16 [64, 2, 2048, 64], P(('groups', 'freq')), parts along dimension 0, may hold values from -0.09375 to 0.09375
- fdmt_offsets: int32 [5, 2, 128], replicated, may hold values from 0 to 63, as said below
- box_lengths: int32 [8], replicated, may hold values from 1 to 64, as said below
Outputs:
- dedispersed: float32 [256, 64, 256], P(('groups', 'freq')), parts along dimension 0
- box_scores: float32 [256, 8, 64], P(('groups', 'freq')), parts along dimension 0
- peak_per_beam: float32 [128], P('groups'), parts along dimension 0
There are 2 independent parts, one for each index of `groups`. A program takes and returns all parts, laid end to end along the dimension named above; an argument that names none is the same for every part. Nothing has to cross between parts.
Inputs may be any that keep to these rules, and one draw needn't show every extreme that they name: `fdmt_offsets`: at level k every entry is below 4 * 2^k. Within each merged subband both rows are nondecreasing in d and rise by at most one per step; their sum is d except where the upper row stops at its largest value. `box_lengths`: the last filter is exactly 64 samples long.
All inputs are finite; a program needn't handle non-finite values.
Results may differ from a plain program's by a relative error of at most 0.0024.
The roundings to bfloat16 on the way count: a program that leaves them out, or rounds other values in their place, can miss the bound.
Values sent between devices are 32-bit elements; how exact they have to be, the bound alone decides.
A program may use at most 64 MiB of HBM per device.

v0:
```python
import math

import jax
import jax.numpy as jnp
from jax import lax
from jax.sharding import PartitionSpec as P


def shift_time(value_array, amount):
    length = value_array.shape[-1]
    if amount >= length:
        return jnp.zeros_like(value_array)
    zeros_part = jnp.zeros(value_array.shape[:-1] + (amount,), value_array.dtype)
    return jnp.concatenate([zeros_part, value_array[..., : length - amount]], axis=-1)


def delay_rows(value_array, lag_rows, child_rows):
    result = value_array
    for section_bit in range(max(child_rows - 1, 0).bit_length()):
        step_size = 1 << section_bit
        chosen = lag_rows >> section_bit & 1 == 1
        result = jnp.where(chosen[:, :, None, None], shift_time(result, step_size), result)
    return result


def take_band(band_rows, row_index):
    return jnp.take(band_rows, row_index, axis=0)


def merge_bands(lower_band, upper_band, low_rows, high_rows):
    child_rows = lower_band.shape[1]
    from_lower = jax.vmap(take_band)(lower_band, low_rows)
    from_upper = delay_rows(jax.vmap(take_band)(upper_band, high_rows), low_rows, child_rows)
    return from_lower + from_upper


def first_plane(cleaned, delay_rate):
    running_sum = cleaned
    term_list = [cleaned]
    for lag_count in range(1, delay_rate):
        running_sum = running_sum + shift_time(cleaned, lag_count)
        term_list.append(running_sum)
    return jnp.stack(term_list, 1)


def normalize(power_rows):
    level_mean = jnp.mean(power_rows, axis=-1, keepdims=True)
    centered = power_rows - level_mean
    spread = jnp.mean(centered * centered, axis=-1, keepdims=True)
    return centered / jnp.sqrt(spread + 1e-05)


def beam_powers(volume, pfb_taps, weight_pair):
    tap_total = pfb_taps.shape[0]
    samples = volume.shape[0] - tap_total + 1
    beam_total = weight_pair.shape[-1]
    filtered = pfb_taps[0][None, :, None, None] * volume[0:samples].astype(jnp.float32)
    for tap_index in range(1, tap_total):
        filtered = filtered + pfb_taps[tap_index][None, :, None, None] * volume[
            tap_index : tap_index + samples
        ].astype(jnp.float32)
    fine_sum = (filtered[:, 0] + filtered[:, 1]).astype(jnp.bfloat16)
    fine_diff = (filtered[:, 0] - filtered[:, 1]).astype(jnp.bfloat16)
    powers = []
    for channel, fine_data in enumerate((fine_sum, fine_diff)):
        weights = weight_pair[channel]
        stacked = jnp.concatenate(
            [
                jnp.concatenate([weights[0], weights[1]], 1),
                jnp.concatenate([-weights[1], weights[0]], 1),
            ],
            0,
        )
        beam_out = jnp.einsum(
            "kb,sk->bs", stacked, fine_data.reshape(samples, -1), preferred_element_type=jnp.float32
        )
        real_part = beam_out[:beam_total]
        imag_part = beam_out[beam_total:]
        powers.append(real_part * real_part + imag_part * imag_part)
    return jnp.stack(powers, 1)


def shards(voltages, pfb_taps, steering, fdmt_offsets, box_lengths):
    devices = lax.axis_size("freq")
    device_id = lax.axis_index("freq")
    beam_total = steering.shape[-1]
    level_count = fdmt_offsets.shape[0]
    delays = fdmt_offsets.shape[-1]
    channels = 2 * devices
    delay_rate = delays // channels
    top_bit = devices.bit_length() - 2
    per_device = 2 * beam_total // devices
    half_rows = delays // 2
    half_index = device_id >> top_bit
    final_rows = lax.dynamic_slice_in_dim(
        fdmt_offsets[level_count - 1], half_index * half_rows, half_rows, axis=1
    )
    normed = normalize(beam_powers(voltages[0], pfb_taps, steering))
    outgoing = jnp.broadcast_to(normed[None], (2,) + normed.shape).reshape(
        devices, per_device, 2, normed.shape[-1]
    )
    incoming = lax.all_to_all(outgoing, "freq", split_axis=0, concat_axis=0, tiled=True)
    by_channel = jnp.transpose(incoming, (0, 2, 1, 3)).reshape(channels, per_device, -1)
    cleaned = by_channel - jnp.mean(by_channel, axis=0, keepdims=True)
    plane_now = first_plane(cleaned, delay_rate)
    for level_index in range(level_count - 1):
        band_count = plane_now.shape[0]
        child_rows = plane_now.shape[1]
        paired = plane_now.reshape(band_count // 2, 2, child_rows, per_device, plane_now.shape[-1])
        level_rows = fdmt_offsets[level_index].reshape(2, band_count // 2, 2 * child_rows)
        plane_now = merge_bands(paired[:, 0], paired[:, 1], level_rows[0], level_rows[1])
    final_plane = merge_bands(plane_now[0:1], plane_now[1:2], final_rows[0:1], final_rows[1:2])[0]
    scaled = final_plane / math.sqrt(channels)
    dedispersed = jnp.transpose(scaled, (1, 0, 2))
    samples = dedispersed.shape[-1]
    running = jnp.cumsum(dedispersed, axis=-1)
    padded = jnp.concatenate([jnp.zeros(running.shape[:-1] + (samples,), jnp.float32), running], -1)
    score_list = []
    for box_index in range(box_lengths.shape[0]):
        box_width = box_lengths[box_index]
        lagged = lax.dynamic_slice_in_dim(padded, samples - box_width, samples, axis=2)
        score_list.append(
            jnp.max((running - lagged) / jnp.sqrt(box_width.astype(jnp.float32)), axis=-1)
        )
    box_scores = jnp.stack(score_list, 1)
    local_best = jnp.max(box_scores, axis=(1, 2))
    beam_start = device_id % (devices // 2) * per_device
    contrib = lax.dynamic_update_slice(
        jnp.full((beam_total,), -1e30, jnp.float32), local_best, (beam_start,)
    )
    peak_per_beam = lax.pmax(contrib, "freq")
    return (dedispersed, box_scores, peak_per_beam)


def solution(mesh):
    placed = (
        P(("groups", "freq"), None, None, None, None),
        P(),
        P(("groups", "freq"), None, None, None),
        P(),
        P(),
    )
    return jax.shard_map(
        shards,
        mesh=mesh,
        in_specs=placed,
        out_specs=(
            P(("groups", "freq"), None, None),
            P(("groups", "freq"), None, None),
            P("groups"),
        ),
        check_vma=False,
    )
```

profile of v0, /device:TPU:0, one launch (start us, length us, event | category | flops | bytes accessed | tf_op | source)
XLA Modules:
  0.0 134.0 jit_solution(6319524763034091593)
XLA Ops:
  0.6 1.3 slice_bitcast_fusion.10
  1.9 1.1 fusion.53
  3.0 1.3 slice_reduce_fusion.7
  4.2 28.8 %fusion = f32[256,2,2,2048]{3,2,1,0:T(2,128)S(1)} fusion(f32[2]{0:T(128)S(1)} %get-tuple-element.47, f32[2]{0:T(128)S(1)} %get-tuple-element.48, f32[2]{0:T(128)S(1)} %get-tuple-element.42, f32[2]{0:T(128)S(1)} %get-tuple-element.43, f32[2]{0:T(128)S(1)} %get-tuple-element.44, f32[2]{0:T(128)S(1)} %get-tuple-element.45, f32[2]{0:T(128)S(1)} %get-tuple-element.46, ...), kind=kLoop, calls=%fused_computation.11 | loop fusion | flops 48234496 | bytes 41943104 | tf_op jit(solution)/shard_map/add | solution.py:59
  33.1 3.9 %add_convert_fusion = (bf16[256,1,2,2048]{3,2,1,0:T(2,128)(2,1)S(1)}, bf16[256,1,2,2048]{3,2,1,0:T(2,128)(2,1)S(1)}) fusion(f32[256,2,2,2048]{3,2,1,0:T(2,128)S(1)} %fusion), kind=kLoop, calls=%fused_computation.26 | loop fusion | flops 4194304 | bytes 12582912 | tf_op jit(solution)/shard_map/convert_element_type | solution.py:62
  36.9 0.9 copy.48
  37.8 0.9 copy.49
  38.8 0.8 fusion.7
  39.6 0.8 fusion.15
  40.9 0.7 copy.37
  41.7 7.4 %all-to-all-start = ((f32[16,8,2,256]{3,1,2,0:T(8,128)}), f32[16,8,2,256]{3,1,2,0:T(8,128)S(1)}, u32[]{:S(2)}, u32[]{:S(2)}) async-start(f32[16,8,2,256]{3,1,2,0:T(8,128)} %copy.37), calls=%async_computation | async-start | bytes 524288 | tf_op jit(solution)/shard_map/all_to_all | solution.py:102
  50.2 0.7 fusion.64
  67.3 0.3 pad_add_fusion
  67.8 1.0 gather_fusion.1
  69.0 0.6 pad_select_fusion.9
  69.7 1.0 gather_fusion
  70.7 0.7 select_add_fusion.3
  71.6 1.0 gather_fusion.3
  72.8 0.6 pad_select_fusion.8
  73.5 0.5 pad_select_fusion.7
  74.0 1.0 gather_fusion.2
  75.0 0.8 select_add_fusion.2
  75.8 1.0 gather_fusion.5
  77.1 0.6 pad_select_fusion.6
  77.8 0.5 pad_select_fusion.5
  78.2 0.5 pad_select_fusion.4
  78.7 1.0 gather_fusion.4
  79.8 1.0 select_add_fusion.1
  80.8 1.0 gather_fusion.7
  82.1 0.6 pad_select_fusion.3
  82.7 0.5 pad_select_fusion.2
  83.2 0.5 pad_select_fusion.1
  83.7 0.5 pad_select_fusion
  84.2 1.0 gather_fusion.6
  85.2 0.8 select_add_fusion
  86.1 0.7 gather_fusion.9
  86.9 0.3 pad_select_fusion.14
  87.2 0.3 pad_select_fusion.13
  87.5 0.3 pad_select_fusion.12
  87.8 0.3 pad_select_fusion.11
  88.3 0.7 gather_fusion.8
  89.0 0.3 fusion.40
  89.5 4.8 %reduce-window.6 = f32[8,64,2,128]{3,1,2,0:T(8,128)S(1)} reduce-window(f32[8,64,2,128]{3,1,2,0:T(8,128)S(1)} %copy.42, f32[]{:T(128)} %constant.60.clone.1), window={size=1x1x1x128 pad=0_0x0_0x0_0x127_0}, to_apply=%region_3.9 | reduce-window | flops 16646144 | bytes 1048580 | tf_op jit(solution)/shard_map/reduce-window
  95.0 1.0 fusion.38
  97.2 0.4 fusion.26
  98.0 34.3 %pmax.7 = f32[64]{0:T(128)} all-reduce(f32[64]{0:T(128)S(1)} %maximum_dynamic-update-slice_fusion), channel_id=1, replica_groups=mesh['groups'=2,'freq'=16] {'freq'}, use_global_device_ids=true, to_apply=%region_21.27 | all-reduce | flops 64 | bytes 512 | tf_op jit(solution)/shard_map/pmax | solution.py:131
  132.4 1.0 copy.46
  133.3 0.7 stack.64
  (86 shorter events, 6.5 us)
Async XLA Ops:
  39.6 9.5 %copy-start.1 = (s32[5,2,128]{2,1,0:T(2,128)S(1)}, s32[5,2,128]{2,1,0:T(2,128)}, u32[]{:S(2)}) copy-start(s32[5,2,128]{2,1,0:T(2,128)} %param.18) | copy-start | bytes 15364
  39.6 10.0 %slice-start = ((s32[5,2,128]{2,1,0:T(2,128)}), s32[1,2,128]{2,1,0:T(2,128)S(1)}, s32[]{:S(2)}) async-start(s32[5,2,128]{2,1,0:T(2,128)} %param.18), calls=%async_computation.1 | async-start | bytes 2048 | tf_op jit(solution)/shard_map/slice | solution.py:96
  39.6 10.6 %copy-start = (s32[8]{0:T(128)S(1)}, s32[8]{0:T(128)}, u32[]{:S(2)}) copy-start(s32[8]{0:T(128)} %param.19) | copy-start | bytes 100
  41.7 25.5 %all-to-all-start = ((f32[16,8,2,256]{3,1,2,0:T(8,128)}), f32[16,8,2,256]{3,1,2,0:T(8,128)S(1)}, u32[]{:S(2)}, u32[]{:S(2)}) async-start(f32[16,8,2,256]{3,1,2,0:T(8,128)} %copy.37), calls=%async_computation | async-start | bytes 524288 | tf_op jit(solution)/shard_map/all_to_all | solution.py:102
where the time goes:
time: 134 us
  other arithmetic  54.1 us (40%)
  blocking collectives  34.3 us (26%)
  local copies, waits for them, and re-layouts  19.7 us (15%)
  between operations  16.8 us (13%)
  starting transfers between devices  7.4 us (6%)
  matrix products  1.67 us (1%)
    pmax x1, blocking collectives, shards(): peak_per_beam = lax.pmax(contrib, 'freq')  34.3 us
    add x1, other arithmetic, beam_powers(): filtered + pfb_taps[tap_index][None, :, None, None] * volume[tap_index:ta...  28.8 us
    gather x23, local copies, waits for them, and re-layouts, take_band(): return jnp.take(band_rows, row_index, axis=0)  10.6 us
    all_to_all x1, starting transfers between devices, shards(): lax.all_to_all(outgoing, 'freq', split_axis=0, concat_axis=0, tiled=True)  7.4 us
    select_n x15, other arithmetic, delay_rows(): jnp.where(chosen[:, :, None, None], shift_time(result, step_size), result)  6.81 us
    another operation x3, other arithmetic  5.04 us
    convert_element_type x1, other arithmetic, beam_powers(): fine_sum = (filtered[:, 0] + filtered[:, 1]).astype(jnp.bfloat16)  3.85 us
    add x4, other arithmetic, merge_bands(): return from_lower + from_upper  3.21 us
  transfers between devices with their start and end apart: 1, of which 0 were waited for; matrix products, arithmetic and copies ran while one was open for 2% of the time, Pallas kernels for 0%

commit v1 on v0

v1 whole, which is shorter than its diff:
```python
import functools
import math

import jax
import jax.numpy as jnp
from jax import lax
from jax.experimental import pallas as pl
from jax.experimental.pallas import tpu as pltpu
from jax.sharding import PartitionSpec as P

MESH = pl.DeviceIdType.MESH
LANES = 128
CHUNK = 512


def unrolled(count, body):
    step = math.gcd(count, 8)

    def several(index, carry):
        for offset in range(step):
            body(index * step + offset)
        return carry

    lax.fori_loop(0, count // step, several, 0)


def shift_tiles(tiles, amount, bound, lane):
    whole, part = 0, amount
    if bound > LANES:
        whole, part = amount // LANES, amount % LANES
    rolled = [pltpu.roll(tile, part, 1) for tile in tiles]
    keep = lane >= part
    zero = jnp.zeros_like(rolled[0])
    moved = [jnp.where(keep, rolled[t], rolled[t - 1] if t else zero) for t in range(len(tiles))]
    if bound <= LANES:
        return moved
    result = []
    for t in range(len(tiles)):
        value = zero
        for back in range(t + 1):
            value = jnp.where(whole == back, moved[t - back], value)
        result.append(value)
    return result


def kernel(
    vol_ref, steer_ref, taps_ref, offs_ref, box_ref,
    ded_ref, score_ref, peak_ref,
    wide, total, outgoing, incoming, normed, plane_a, plane_b, final, best_out, best_in,
    send_sems, recv_sems, best_send, best_recv,
):
    devices = lax.axis_size("freq")
    me = lax.axis_index("freq")
    tap_total = taps_ref.shape[0]
    antennas = steer_ref.shape[2]
    beams = steer_ref.shape[3]
    blocks = outgoing.shape[0]
    parts, per = outgoing.shape[1], outgoing.shape[3]
    samples = blocks * LANES
    reach = vol_ref.shape[0] - samples + LANES
    channels = 2 * devices
    levels, _, delays = offs_ref.shape
    rate = delays // channels
    half = delays // 2

    def target(step):
        return lax.rem(me + step, devices)

    barrier = pltpu.get_barrier_semaphore()

    def greet(step, carry):
        pl.semaphore_signal(barrier, 1, device_id={"freq": target(step)}, device_id_type=MESH)
        return carry

    lax.fori_loop(1, devices, greet, 0)

    for channel in range(2):
        wide[channel] = jnp.concatenate([steer_ref[channel, 0], steer_ref[channel, 1]], 1)

    ahead = lax.broadcasted_iota(jnp.int32, (LANES, reach), 1) - lax.broadcasted_iota(
        jnp.int32, (LANES, reach), 0
    )
    bands = []
    for branch in range(2):
        band = jnp.zeros((LANES, reach), jnp.float32)
        for tap in range(tap_total):
            band = jnp.where(ahead == tap, taps_ref[tap, branch], band)
        high = band.astype(jnp.bfloat16)
        low = (band - high.astype(jnp.float32)).astype(jnp.bfloat16)
        bands.append(jnp.concatenate([high, low], 0))

    def copy_block(block, step):
        other = target(step)
        return pltpu.make_async_remote_copy(
            src_ref=outgoing.at[block, lax.rem(other, parts)],
            dst_ref=incoming.at[block, me],
            send_sem=send_sems.at[block, step],
            recv_sem=recv_sems.at[block, me],
            device_id={"freq": other},
            device_id_type=MESH,
        )

    lane_sign = jnp.where(
        lax.broadcasted_iota(jnp.int32, (LANES, 2 * beams), 1) < beams, -1.0, 1.0
    ).astype(jnp.float32)

    for block in range(blocks):
        rows = pl.ds(block * LANES, reach)
        for start in range(0, antennas, CHUNK):
            fine = [[], []]
            for part in range(2):
                filtered = []
                for branch in range(2):
                    column = (2 * branch + part) * antennas + start
                    both = jnp.dot(
                        bands[branch],
                        vol_ref[rows, pl.ds(column, CHUNK)],
                        preferred_element_type=jnp.float32,
                    )
                    filtered.append(both[:LANES] + both[LANES:])
                fine[0].append((filtered[0] + filtered[1]).astype(jnp.bfloat16))
                fine[1].append((filtered[0] - filtered[1]).astype(jnp.bfloat16))
            for channel in range(2):
                product = jnp.dot(
                    jnp.concatenate(fine[channel], 0),
                    wide[channel, pl.ds(start, CHUNK), :],
                    preferred_element_type=jnp.float32,
                )
                if start:
                    total[channel] += product
                else:
                    total[channel] = product
        for channel in range(2):
            beam = total[channel, :LANES] + lane_sign * pltpu.roll(
                total[channel, LANES:], beams, 1
            )
            squares = jnp.transpose(beam * beam)
            power = squares[:beams] + squares[beams:]
            for index in range(parts):
                outgoing[block, index, channel] = power[index * per : (index + 1) * per]
        if block == 0:
            pl.semaphore_wait(barrier, devices - 1)

        def send(step, carry, block=block):
            copy_block(block, step).start()
            return carry

        lax.fori_loop(1, devices, send, 0)
        incoming[block, me] = outgoing[block, lax.rem(me, parts)]

    lane = lax.broadcasted_iota(jnp.int32, (per, LANES), 1)

    for block in range(blocks):

        def receive(step, carry, block=block):
            source = target(step)
            pltpu.make_async_remote_copy(
                src_ref=outgoing.at[block, 0],
                dst_ref=incoming.at[block, source],
                send_sem=send_sems.at[block, step],
                recv_sem=recv_sems.at[block, source],
                device_id={"freq": source},
                device_id_type=MESH,
            ).wait_recv()
            return carry

        lax.fori_loop(1, devices, receive, 0)

    power = [incoming[t].reshape(channels, per, LANES) for t in range(blocks)]
    level = sum(jnp.sum(tile, axis=-1, keepdims=True) for tile in power) / samples
    power = [tile - level for tile in power]
    spread = sum(jnp.sum(tile * tile, axis=-1, keepdims=True) for tile in power) / samples
    inverse = 1.0 / jnp.sqrt(spread + 1e-05)
    for t in range(blocks):
        tile = power[t] * inverse
        normed[t] = tile - jnp.sum(tile, axis=0, keepdims=True) / channels

    def spread_channel(channel):
        tiles = [normed[t, channel] for t in range(blocks)]
        running = tiles
        for lag in range(rate):
            if lag:
                moved = shift_tiles(tiles, lag, LANES, lane)
                running = [running[t] + moved[t] for t in range(blocks)]
            for t in range(blocks):
                plane_a[t, channel * rate + lag] = running[t]

    unrolled(channels, spread_channel)

    def merge_row(plane, level_index, child, row):
        base = row // (2 * child) * (2 * child)
        low = offs_ref[level_index, 0, row]
        high = offs_ref[level_index, 1, row]
        upper = [plane[t, base + child + high] for t in range(blocks)]
        moved = shift_tiles(upper, low, child, lane)
        return [plane[t, base + low] + moved[t] for t in range(blocks)]

    now, later = plane_a, plane_b
    for level_index in range(levels - 1):

        def merge(row, now=now, later=later, level_index=level_index):
            merged = merge_row(now, level_index, rate << level_index, row)
            for t in range(blocks):
                later[t, row] = merged[t]

        unrolled(delays, merge)
        now, later = later, now

    first_row = me // parts * half

    def merge_last(row):
        merged = merge_row(now, levels - 1, half, first_row + row)
        for t in range(blocks):
            final[t, pl.ds(row * per, per), :] = merged[t] * (1.0 / math.sqrt(channels))

    unrolled(half, merge_last)
    for index in range(per):
        for t in range(blocks):
            take = pl.ds(index, half, stride=per) if per > 1 else pl.ds(0, half)
            ded_ref[index, :, t * LANES : (t + 1) * LANES] = final[t, take, :]

    columns = jnp.transpose(ded_ref[...].reshape(per * half, samples))
    high = columns.astype(jnp.bfloat16)
    low = (columns - high.astype(jnp.float32)).astype(jnp.bfloat16)
    pair = jnp.concatenate([high, low], 0)
    behind = lax.broadcasted_iota(jnp.int32, (samples, samples), 0) - lax.broadcasted_iota(
        jnp.int32, (samples, samples), 1
    )
    scores = []
    for index in range(box_ref.shape[0]):
        width = box_ref[index]
        window = jnp.where((behind >= 0) & (behind < width), 1.0, 0.0).astype(jnp.bfloat16)
        sums = jnp.dot(
            jnp.concatenate([window, window], 1), pair, preferred_element_type=jnp.float32
        )
        root = jnp.sqrt(jnp.full((1, per * half), width.astype(jnp.float32)))
        scores.append(jnp.max(sums, axis=0, keepdims=True) / root)
    scores = jnp.concatenate(scores, 0)
    lane = lax.broadcasted_iota(jnp.int32, best_out.shape, 1)
    best = jnp.full(best_out.shape, jnp.finfo(jnp.float32).min, jnp.float32)
    for index in range(per):
        mine = scores[:, index * half : (index + 1) * half]
        score_ref[index] = mine
        peak = jnp.max(jnp.max(mine, axis=1, keepdims=True), axis=0, keepdims=True)
        best = jnp.where(lane == lax.rem(me, parts) * per + index, peak, best)
    best_out[...] = best
    best_in[me] = best

    def copy_best(step, source):
        return pltpu.make_async_remote_copy(
            src_ref=best_out,
            dst_ref=best_in.at[source],
            send_sem=best_send.at[step],
            recv_sem=best_recv.at[source],
            device_id={"freq": target(step)},
            device_id_type=MESH,
        )

    def send_best(step, carry):
        copy_best(step, me).start()
        return carry

    def receive_best(step, carry):
        copy_best(step, target(step)).wait_recv()
        return carry

    def drain(step, carry):
        for block in range(blocks):
            copy_block(block, step).wait_send()
        copy_best(step, me).wait_send()
        return carry

    lax.fori_loop(1, devices, send_best, 0)
    lax.fori_loop(1, devices, receive_best, 0)
    peaks = jnp.max(best_in[...], axis=0)
    peak_ref[...] = peaks[:1, :beams]
    lax.fori_loop(1, devices, drain, 0)


def shards(voltages, pfb_taps, steering, fdmt_offsets, box_lengths):
    devices = lax.axis_size("freq")
    inputs, branches, pair, antennas = voltages.shape[1:]
    tap_total = pfb_taps.shape[0]
    samples = inputs - tap_total + 1
    beams = steering.shape[-1]
    levels, _, delays = fdmt_offsets.shape
    boxes = box_lengths.shape[0]
    per = 2 * beams // devices
    half = delays // 2
    channels = 2 * devices
    blocks = samples // LANES
    reach = -(-(tap_total - 1) // 16) * 16
    volume = jnp.pad(
        voltages.reshape(inputs, branches * pair * antennas),
        ((0, samples + reach - inputs), (0, 0)),
    )
    vmem = pl.BlockSpec(memory_space=pltpu.VMEM)
    smem = pl.BlockSpec(memory_space=pltpu.SMEM)
    f32 = jnp.float32
    dedispersed, box_scores, peaks = pl.pallas_call(
        kernel,
        out_shape=(
            jax.ShapeDtypeStruct((per, half, samples), f32),
            jax.ShapeDtypeStruct((per, boxes, half), f32),
            jax.ShapeDtypeStruct((1, beams), f32),
        ),
        in_specs=[vmem, vmem, smem, smem, smem],
        out_specs=(vmem, vmem, vmem),
        scratch_shapes=[
            pltpu.VMEM((2, antennas, 2 * beams), jnp.bfloat16),
            pltpu.VMEM((2, 2 * LANES, 2 * beams), f32),
            pltpu.VMEM((blocks, beams // per, 2, per, LANES), f32),
            pltpu.VMEM((blocks, devices, 2, per, LANES), f32),
            pltpu.VMEM((blocks, channels, per, LANES), f32),
            pltpu.VMEM((blocks, delays, per, LANES), f32),
            pltpu.VMEM((blocks, delays, per, LANES), f32),
            pltpu.VMEM((blocks, half * per, LANES), f32),
            pltpu.VMEM((8, LANES), f32),
            pltpu.VMEM((devices, 8, LANES), f32),
            pltpu.SemaphoreType.DMA((blocks, devices)),
            pltpu.SemaphoreType.DMA((blocks, devices)),
            pltpu.SemaphoreType.DMA((devices,)),
            pltpu.SemaphoreType.DMA((devices,)),
        ],
        compiler_params=pltpu.CompilerParams(
            collective_id=0, has_side_effects=True, vmem_limit_bytes=48 * 1024 * 1024
        ),
    )(volume, steering, pfb_taps, fdmt_offsets, box_lengths)
    return dedispersed, box_scores, peaks.reshape(beams)


def solution(mesh):
    placed = (
        P(("groups", "freq"), None, None, None, None),
        P(),
        P(("groups", "freq"), None, None, None),
        P(),
        P(),
    )
    return jax.shard_map(
        shards,
        mesh=mesh,
        in_specs=placed,
        out_specs=(
            P(("groups", "freq"), None, None),
            P(("groups", "freq"), None, None),
            P("groups"),
        ),
        check_vma=False,
    )
```

time: 134 us -> 52.2 us (0.39)
  other arithmetic: 54.1 us -> 0 us
  blocking collectives: 34.3 us -> 0 us
  Pallas kernels: 0 us -> 32.5 us
  between operations: 16.8 us -> 0.66 us
  starting transfers between devices: 7.4 us -> 0 us
  matrix products: 1.67 us -> 0 us
    pmax x1 -> x0, blocking collectives: 34.3 us -> none  [shards(): peak_per_beam = lax.pmax(contrib, 'freq')]
    pallas_call x0 -> x1, Pallas kernels: none -> 32.5 us  [shards(): pl.pallas_call(kernel, out_shape=(jax.ShapeDtypeStruct((per, half, sample...]
    add x6 -> x0, other arithmetic: 32.3 us -> none  [the longest x1 28.8 us: beam_powers(): filtered + pfb_taps[tap_index][None, :, None, None] * volume[tap_index:ta...]
    gather x23 -> x0, local copies, waits for them, and re-layouts: 10.6 us -> none  [take_band(): return jnp.take(band_rows, row_index, axis=0)]
    reshape x2 -> x1, local copies, waits for them, and re-layouts: 0.9 us -> 10.7 us  [shards(): voltages.reshape(inputs, branches * pair * antennas)]
    select_n x20 -> x0, other arithmetic: 7.75 us -> none  [the longest x15 6.81 us: delay_rows(): jnp.where(chosen[:, :, None, None], shift_time(result, step_size), result)]
    all_to_all x1 -> x0, starting transfers between devices: 7.4 us -> none  [shards(): lax.all_to_all(outgoing, 'freq', split_axis=0, concat_axis=0, tiled=True)]
    another operation x5 -> x0, other arithmetic: 5.17 us -> none
  transfers between devices with their start and end apart: 1 -> 0, of which waited for: 0 -> 0; matrix products, arithmetic and copies ran while one was open for 2% -> 0% of each run, Pallas kernels for 0% -> 0%
where the time goes in v1:
time: 52.2 us; the launch traced here: 51.8 us
  Pallas kernels  32.5 us (62%)
  local copies, waits for them, and re-layouts  18.7 us (36%)
  between operations  0.66 us (1%)
    pallas_call x1, Pallas kernels, shards(): pl.pallas_call(kernel, out_shape=(jax.ShapeDtypeStruct((per, half, sample...  32.5 us
    reshape x1, local copies, waits for them, and re-layouts, shards(): voltages.reshape(inputs, branches * pair * antennas)  10.7 us
    pad x1, local copies, waits for them, and re-layouts, shards(): jnp.pad(voltages.reshape(inputs, branches * pair * antennas), ((0, sample...  4.92 us
    unnamed x13, local copies, waits for them, and re-layouts  3.08 us

profile of v1, /device:TPU:0, one launch (start us, length us, event | category | flops | bytes accessed | tf_op | source)
XLA Modules:
  0.0 51.8 jit_solution(12074382427300254528)
XLA Ops:
  0.6 10.7 %reshape.12 = bf16[263,8192]{1,0:T(8,128)(2,1)} reshape(bf16[1,263,2,2,2048]{4,3,2,1,0:T(2,128)(2,1)} %param.5) | data formatting | bytes 8617984 | tf_op jit(solution)/shard_map/reshape | solution.py:294
  11.3 0.0 copy-start.2
  11.3 0.0 copy-start.3
  11.3 0.0 copy-start
  11.3 0.0 copy-start.1
  11.3 4.9 %pad.4.vol_ref = bf16[272,8192]{1,0:T(8,128)(2,1)} pad(bf16[263,8192]{1,0:T(8,128)(2,1)} %reshape.12, bf16[]{:T(256)} %constant.2.clone.1), padding=0_9x0_0 | pad | bytes 8765442 | tf_op jit(solution)/shard_map/jit(_pad)/pad | solution.py:293
  16.2 0.0 copy-done.2
  16.2 1.1 %copy.8.steer_ref = bf16[2,2,2048,64]{3,2,1,0:T(8,128)(2,1)S(1)} copy(bf16[2,2,2048,64]{2,3,1,0:T(8,128)(2,1)S(1)} %copy-done.2) | data formatting | bytes 2097152 | tf_op args[2]
  17.3 0.0 copy-done.3
  17.3 0.1 copy.9.taps_ref
  17.4 0.0 copy-done
  17.4 0.0 copy-done.1
  17.4 32.5 %shard_map.76 = (f32[8,64,256]{2,1,0:T(8,128)S(1)}, f32[8,8,64]{2,1,0:T(8,128)S(1)}, f32[1,64]{1,0:T(1,128)S(1)}) custom-call(bf16[272,8192]{1,0:T(8,128)(2,1)} %pad.4.vol_ref, bf16[2,2,2048,64]{3,2,1,0:T(8,128)(2,1)S(1)} %copy.8.steer_ref, f32[8,2]{1,0:T(8,128)S(1)} %copy.9.taps_ref, s32[5,2,128]{2,1,0:T(2,128)S(1)} %copy-done, s32[8]{0:T(128)S(1)} %copy-done.1), custom_call_target="tpu_custom_call" | custom-call | tf_op jit(solution)/shard_map/pallas_call | solution.py:300
  49.9 0.8 %copy.13 = f32[8,64,256]{2,1,0:T(8,128)} copy(f32[8,64,256]{2,1,0:T(8,128)S(1)} %get-tuple-element.12) | data formatting | bytes 1048576
  50.7 0.6 %copy.14 = f32[8,8,64]{2,1,0:T(8,128)} copy(f32[8,8,64]{2,1,0:T(8,128)S(1)} %get-tuple-element.13) | data formatting | bytes 32768
  51.3 0.5 copy.15
Async XLA Ops:
  11.3 4.9 %copy-start.2 = (bf16[2,2,2048,64]{2,3,1,0:T(8,128)(2,1)S(1)}, bf16[2,2,2048,64]{2,3,1,0:T(8,128)(2,1)}, u32[]{:S(2)}) copy-start(bf16[2,2,2048,64]{2,3,1,0:T(8,128)(2,1)} %param.7) | copy-start | bytes 3145732
  11.3 6.0 %copy-start.3 = (f32[8,2]{0,1:T(2,128)S(1)}, f32[8,2]{0,1:T(2,128)}, u32[]{:S(2)}) copy-start(f32[8,2]{0,1:T(2,128)} %param.6) | copy-start | bytes 196
  11.3 6.1 %copy-start = (s32[5,2,128]{2,1,0:T(2,128)S(1)}, s32[5,2,128]{2,1,0:T(2,128)}, u32[]{:S(2)}) copy-start(s32[5,2,128]{2,1,0:T(2,128)} %offs_ref.1) | copy-start | bytes 15364
  11.3 6.1 %copy-start.1 = (s32[8]{0:T(128)S(1)}, s32[8]{0:T(128)}, u32[]{:S(2)}) copy-start(s32[8]{0:T(128)} %box_ref.1) | copy-start | bytes 100

commit v2 on v1

v2 whole, which is shorter than its diff:
```python
import functools
import math

import jax
import jax.numpy as jnp
from jax import lax
from jax.experimental import pallas as pl
from jax.experimental.pallas import tpu as pltpu
from jax.sharding import PartitionSpec as P

MESH = pl.DeviceIdType.MESH
LANES = 128
SHORT = 64
CHUNK = 512
GRANT = 48 * 1024 * 1024


def unrolled(count, body):
    step = math.gcd(count, 32)

    def several(index, carry):
        for offset in range(step):
            body(index * step + offset)
        return carry

    lax.fori_loop(0, count // step, several, 0)


def shift_tiles(tiles, amount, bound, lane):
    whole, part = 0, amount
    if bound > LANES:
        whole, part = amount // LANES, amount % LANES
    rolled = [pltpu.roll(tile, part, 1) for tile in tiles]
    keep = lane >= part
    zero = jnp.zeros_like(rolled[0])
    moved = [jnp.where(keep, rolled[t], rolled[t - 1] if t else zero) for t in range(len(tiles))]
    if bound <= LANES:
        return moved
    result = []
    for t in range(len(tiles)):
        value = zero
        for back in range(t + 1):
            value = jnp.where(whole == back, moved[t - back], value)
        result.append(value)
    return result


def targets(me, devices):
    return lambda step: lax.rem(me + step, devices)


def greet_all(target, devices):
    barrier = pltpu.get_barrier_semaphore()

    def greet(step, carry):
        pl.semaphore_signal(barrier, 1, device_id={"freq": target(step)}, device_id_type=MESH)
        return carry

    lax.fori_loop(1, devices, greet, 0)
    return barrier


def each_other(devices, body):
    def step_body(step, carry):
        body(step)
        return carry

    lax.fori_loop(1, devices, step_body, 0)


def channel_kernel(
    vol_ref, steer_ref, taps_ref, clean_ref,
    tiles, wide, total, outgoing, incoming, tile_sems, send_sems, recv_sems,
):
    devices = lax.axis_size("freq")
    me = lax.axis_index("freq")
    tap_total = taps_ref.shape[1]
    inputs, branches = vol_ref.shape[:2]
    beams, antennas = steer_ref.shape[2:]
    blocks = outgoing.shape[0]
    parts, per = outgoing.shape[1], outgoing.shape[3]
    samples = blocks * LANES
    channels = 2 * devices
    columns = antennas // LANES
    padded = tiles.shape[1]
    reach = 2 * (SHORT + padded - samples)
    target = targets(me, devices)
    barrier = greet_all(target, devices)

    def tile_copy(index):
        return pltpu.make_async_copy(
            vol_ref.at[:, index % branches, :, pl.ds(index // branches * LANES, LANES)],
            tiles.at[index, pl.ds(0, inputs)],
            tile_sems.at[index],
        )

    def flat(index):
        return tiles.at[index].reshape(2 * padded, LANES)

    for index in range(branches * columns):
        flat(index)[2 * samples :, :] = jnp.zeros((2 * padded - 2 * samples, LANES), jnp.bfloat16)
        tile_copy(index).start()

    for channel in range(2):
        wide[channel] = jnp.transpose(
            jnp.concatenate([steer_ref[channel, 0], steer_ref[channel, 1]], 0)
        )

    row = lax.broadcasted_iota(jnp.int32, (SHORT, reach), 0)
    column = lax.broadcasted_iota(jnp.int32, (SHORT, reach), 1)
    bands = []
    for branch in range(branches):
        pieces = []
        for part in range(2):
            band = jnp.zeros((SHORT, reach), jnp.float32)
            for tap in range(tap_total):
                band = jnp.where(column == 2 * (row + tap) + part, taps_ref[branch, tap], band)
            high = band.astype(jnp.bfloat16)
            pieces += [high, (band - high.astype(jnp.float32)).astype(jnp.bfloat16)]
        bands.append(jnp.concatenate(pieces, 0))

    def copy_block(block, step, source):
        other = target(step)
        return pltpu.make_async_remote_copy(
            src_ref=outgoing.at[block, lax.rem(other, parts)],
            dst_ref=incoming.at[block, source],
            send_sem=send_sems.at[block, step],
            recv_sem=recv_sems.at[block, source],
            device_id={"freq": other},
            device_id_type=MESH,
        )

    lane_sign = jnp.where(
        lax.broadcasted_iota(jnp.int32, (LANES, 2 * beams), 1) < beams, -1.0, 1.0
    ).astype(jnp.float32)

    for block in range(blocks):
        for start in range(0, antennas, CHUNK):
            first = start // LANES
            if block == 0:
                for index in range(first * branches, (first + CHUNK // LANES) * branches):
                    tile_copy(index).wait()
            fine = [[[], []], [[], []]]
            for short in range(0, LANES, SHORT):
                rows = pl.ds(2 * (block * LANES + short), reach)
                filtered = []
                for branch in range(branches):
                    volume = jnp.concatenate(
                        [
                            flat((first + tile) * branches + branch)[rows, :]
                            for tile in range(CHUNK // LANES)
                        ],
                        1,
                    )
                    both = jnp.dot(bands[branch], volume, preferred_element_type=jnp.float32)
                    filtered.append(
                        [
                            both[2 * part * SHORT : (2 * part + 1) * SHORT]
                            + both[(2 * part + 1) * SHORT : (2 * part + 2) * SHORT]
                            for part in range(2)
                        ]
                    )
                for part in range(2):
                    even, odd = filtered[0][part], filtered[1][part]
                    fine[0][part].append((even + odd).astype(jnp.bfloat16))
                    fine[1][part].append((even - odd).astype(jnp.bfloat16))
            for channel in range(2):
                product = jnp.dot(
                    jnp.concatenate(fine[channel][0] + fine[channel][1], 0),
                    wide[channel, pl.ds(start, CHUNK), :],
                    preferred_element_type=jnp.float32,
                )
                if start:
                    total[channel] += product
                else:
                    total[channel] = product
        for channel in range(2):
            beam = total[channel, :LANES] + lane_sign * pltpu.roll(
                total[channel, LANES:], beams, 1
            )
            squares = jnp.transpose(beam * beam)
            power = squares[:beams] + squares[beams:]
            for index in range(parts):
                outgoing[block, index, channel] = power[index * per : (index + 1) * per]
        if block == 0:
            pl.semaphore_wait(barrier, devices - 1)
        each_other(devices, lambda step, block=block: copy_block(block, step, me).start())
        incoming[block, me] = outgoing[block, lax.rem(me, parts)]

    for block in range(blocks):
        each_other(
            devices, lambda step, block=block: copy_block(block, step, target(step)).wait_recv()
        )

    power = [incoming[t].reshape(channels, per, LANES) for t in range(blocks)]
    level = sum(jnp.sum(tile, axis=-1, keepdims=True) for tile in power) / samples
    power = [tile - level for tile in power]
    spread = sum(jnp.sum(tile * tile, axis=-1, keepdims=True) for tile in power) / samples
    inverse = 1.0 / jnp.sqrt(spread + 1e-05)
    for t in range(blocks):
        tile = power[t] * inverse
        clean_ref[t] = tile - jnp.sum(tile, axis=0, keepdims=True) / channels

    def drain(step):
        for block in range(blocks):
            copy_block(block, step, me).wait_send()

    each_other(devices, drain)


def tree_kernel(
    clean_ref, offs_ref, box_ref, ded_ref, score_ref, best_ref, plane_a, plane_b, final
):
    devices = lax.axis_size("freq")
    me = lax.axis_index("freq")
    blocks, channels, per, _ = clean_ref.shape
    parts = devices // 2
    samples = blocks * LANES
    levels, _, delays = offs_ref.shape
    rate = delays // channels
    half = delays // 2
    lane = lax.broadcasted_iota(jnp.int32, (per, LANES), 1)

    def spread_channel(channel):
        tiles = [clean_ref[t, channel] for t in range(blocks)]
        running = tiles
        for lag in range(rate):
            if lag:
                moved = shift_tiles(tiles, lag, LANES, lane)
                running = [running[t] + moved[t] for t in range(blocks)]
            for t in range(blocks):
                plane_a[t, channel * rate + lag] = running[t]

    unrolled(channels, spread_channel)

    def merge_row(plane, level_index, child, row):
        base = row // (2 * child) * (2 * child)
        low = offs_ref[level_index, 0, row]
        high = offs_ref[level_index, 1, row]
        upper = [plane[t, base + child + high] for t in range(blocks)]
        moved = shift_tiles(upper, low, child, lane)
        return [plane[t, base + low] + moved[t] for t in range(blocks)]

    now, later = plane_a, plane_b
    for level_index in range(levels - 1):

        def merge(row, now=now, later=later, level_index=level_index):
            merged = merge_row(now, level_index, rate << level_index, row)
            for t in range(blocks):
                later[t, row] = merged[t]

        unrolled(delays, merge)
        now, later = later, now

    first_row = me // parts * half

    def merge_last(row):
        merged = merge_row(now, levels - 1, half, first_row + row)
        for t in range(blocks):
            final[t, pl.ds(row * per, per), :] = merged[t] * (1.0 / math.sqrt(channels))

    unrolled(half, merge_last)
    for index in range(per):
        for t in range(blocks):
            take = pl.ds(index, half, stride=per) if per > 1 else pl.ds(0, half)
            ded_ref[index, :, t * LANES : (t + 1) * LANES] = final[t, take, :]

    columns = jnp.transpose(ded_ref[...].reshape(per * half, samples))
    high = columns.astype(jnp.bfloat16)
    low = (columns - high.astype(jnp.float32)).astype(jnp.bfloat16)
    pair = jnp.concatenate([high, low], 0)
    behind = lax.broadcasted_iota(jnp.int32, (samples, samples), 0) - lax.broadcasted_iota(
        jnp.int32, (samples, samples), 1
    )
    scores = []
    for index in range(box_ref.shape[0]):
        width = box_ref[index]
        window = jnp.where((behind >= 0) & (behind < width), 1.0, 0.0).astype(jnp.bfloat16)
        sums = jnp.dot(
            jnp.concatenate([window, window], 1), pair, preferred_element_type=jnp.float32
        )
        root = jnp.sqrt(jnp.full((1, per * half), width.astype(jnp.float32)))
        scores.append(jnp.max(sums, axis=0, keepdims=True) / root)
    scores = jnp.concatenate(scores, 0)
    lane = lax.broadcasted_iota(jnp.int32, best_ref.shape, 1)
    best = jnp.full(best_ref.shape, jnp.finfo(jnp.float32).min, jnp.float32)
    for index in range(per):
        mine = scores[:, index * half : (index + 1) * half]
        score_ref[index] = mine
        peak = jnp.max(jnp.max(mine, axis=1, keepdims=True), axis=0, keepdims=True)
        best = jnp.where(lane == lax.rem(me, parts) * per + index, peak, best)
    best_ref[...] = best


def peak_kernel(best_ref, peak_ref, best_in, best_send, best_recv):
    devices = lax.axis_size("freq")
    me = lax.axis_index("freq")
    target = targets(me, devices)
    barrier = greet_all(target, devices)
    best_in[me] = best_ref[...]
    pl.semaphore_wait(barrier, devices - 1)

    def copy_best(step, source):
        return pltpu.make_async_remote_copy(
            src_ref=best_ref,
            dst_ref=best_in.at[source],
            send_sem=best_send.at[step],
            recv_sem=best_recv.at[source],
            device_id={"freq": target(step)},
            device_id_type=MESH,
        )

    each_other(devices, lambda step: copy_best(step, me).start())
    each_other(devices, lambda step: copy_best(step, target(step)).wait_recv())
    peaks = jnp.max(best_in[...], axis=0)
    peak_ref[...] = peaks[:1, : peak_ref.shape[1]]
    each_other(devices, lambda step: copy_best(step, me).wait_send())


def shards(voltages, pfb_taps, steering, fdmt_offsets, box_lengths):
    devices = lax.axis_size("freq")
    inputs, branches, pair, antennas = voltages.shape[1:]
    tap_total = pfb_taps.shape[0]
    samples = inputs - tap_total + 1
    beams = steering.shape[-1]
    levels, _, delays = fdmt_offsets.shape
    boxes = box_lengths.shape[0]
    per = 2 * beams // devices
    half = delays // 2
    channels = 2 * devices
    blocks = samples // LANES
    padded = samples + -(-(tap_total - 1) // 8) * 8
    tile_total = branches * antennas // LANES
    vmem = pl.BlockSpec(memory_space=pltpu.VMEM)
    smem = pl.BlockSpec(memory_space=pltpu.SMEM)
    f32 = jnp.float32
    cleaned = pl.pallas_call(
        channel_kernel,
        out_shape=jax.ShapeDtypeStruct((blocks, channels, per, LANES), f32),
        in_specs=[pl.BlockSpec(memory_space=pl.ANY), vmem, smem],
        out_specs=vmem,
        scratch_shapes=[
            pltpu.VMEM((tile_total, padded, pair, LANES), jnp.bfloat16),
            pltpu.VMEM((2, antennas, 2 * beams), jnp.bfloat16),
            pltpu.VMEM((2, 2 * LANES, 2 * beams), f32),
            pltpu.VMEM((blocks, beams // per, 2, per, LANES), f32),
            pltpu.VMEM((blocks, devices, 2, per, LANES), f32),
            pltpu.SemaphoreType.DMA((tile_total,)),
            pltpu.SemaphoreType.DMA((blocks, devices)),
            pltpu.SemaphoreType.DMA((blocks, devices)),
        ],
        compiler_params=pltpu.CompilerParams(
            collective_id=0, has_side_effects=True, vmem_limit_bytes=GRANT
        ),
    )(voltages[0], jnp.transpose(steering, (0, 1, 3, 2)), pfb_taps.T)
    dedispersed, box_scores, best = pl.pallas_call(
        tree_kernel,
        out_shape=(
            jax.ShapeDtypeStruct((per, half, samples), f32),
            jax.ShapeDtypeStruct((per, boxes, half), f32),
            jax.ShapeDtypeStruct((8, LANES), f32),
        ),
        in_specs=[vmem, smem, smem],
        out_specs=(vmem, vmem, vmem),
        scratch_shapes=[
            pltpu.VMEM((blocks, delays, per, LANES), f32),
            pltpu.VMEM((blocks, delays, per, LANES), f32),
            pltpu.VMEM((blocks, half * per, LANES), f32),
        ],
        compiler_params=pltpu.CompilerParams(vmem_limit_bytes=GRANT),
    )(cleaned, fdmt_offsets, box_lengths)
    peaks = pl.pallas_call(
        peak_kernel,
        out_shape=jax.ShapeDtypeStruct((1, beams), f32),
        in_specs=[vmem],
        out_specs=vmem,
        scratch_shapes=[
            pltpu.VMEM((devices, 8, LANES), f32),
            pltpu.SemaphoreType.DMA((devices,)),
            pltpu.SemaphoreType.DMA((devices,)),
        ],
        compiler_params=pltpu.CompilerParams(collective_id=1, has_side_effects=True),
    )(best)
    return dedispersed, box_scores, peaks.reshape(beams)


def solution(mesh):
    placed = (
        P(("groups", "freq"), None, None, None, None),
        P(),
        P(("groups", "freq"), None, None, None),
        P(),
        P(),
    )
    return jax.shard_map(
        shards,
        mesh=mesh,
        in_specs=placed,
        out_specs=(
            P(("groups", "freq"), None, None),
            P(("groups", "freq"), None, None),
            P("groups"),
        ),
        check_vma=False,
    )
```

time: 52.2 us -> 44.1 us (0.84)
  local copies, waits for them, and re-layouts: 18.7 us -> 5.84 us
  Pallas kernels: 32.5 us -> 37.4 us
    reshape x1 -> x0, local copies, waits for them, and re-layouts: 10.7 us -> none  [shards(): voltages.reshape(inputs, branches * pair * antennas)]
    pad x1 -> x0, local copies, waits for them, and re-layouts: 4.92 us -> none  [shards(): jnp.pad(voltages.reshape(inputs, branches * pair * antennas), ((0, sample...]
    pallas_call x1 -> x3, Pallas kernels: 32.5 us -> 37.4 us  [the longest x1 20.2 us: shards(): pl.pallas_call(channel_kernel, out_shape=jax.ShapeDtypeStruct((blocks, ch...]
    unnamed x13, local copies, waits for them, and re-layouts: 3.08 us -> 5.84 us
where the time goes in v2:
time: 44.1 us; the launch traced here: 43.9 us
  Pallas kernels  37.4 us (85%)
  local copies, waits for them, and re-layouts  5.84 us (13%)
  between operations  0.69 us (2%)
    pallas_call x1, Pallas kernels, shards(): pl.pallas_call(channel_kernel, out_shape=jax.ShapeDtypeStruct((blocks, ch...  20.2 us
    pallas_call x1, Pallas kernels, shards(): pl.pallas_call(tree_kernel, out_shape=(jax.ShapeDtypeStruct((per, half, s...  9.17 us
    pallas_call x1, Pallas kernels, shards(): pl.pallas_call(peak_kernel, out_shape=jax.ShapeDtypeStruct((1, beams), f3...  8.03 us
    unnamed x13, local copies, waits for them, and re-layouts  5.84 us

profile of v2, /device:TPU:0, one launch (start us, length us, event | category | flops | bytes accessed | tf_op | source)
XLA Modules:
  0.0 43.9 jit_solution(5581442479437997288)
XLA Ops:
  0.6 0.0 copy-start.5
  0.6 0.0 copy-start.2
  0.7 0.0 copy-start
  0.7 2.2 %copy-done = bf16[1,263,2,2,2048]{4,3,2,1,0:T(2,128)(2,1)S(1)} copy-done((bf16[1,263,2,2,2048]{4,3,2,1,0:T(2,128)(2,1)S(1)}, bf16[1,263,2,2,2048]{4,3,2,1,0:T(2,128)(2,1)}, u32[]{:S(2)}) %copy-start) | copy-done | bytes 4309016
  2.9 0.0 copy-start.1
  2.9 1.2 %copy-done.1 = bf16[2,2,2048,64]{2,3,1,0:T(8,128)(2,1)S(1)} copy-done((bf16[2,2,2048,64]{2,3,1,0:T(8,128)(2,1)S(1)}, bf16[2,2,2048,64]{2,3,1,0:T(8,128)(2,1)}, u32[]{:S(2)}) %copy-start.1) | copy-done | bytes 1048600
  4.1 0.0 copy-start.4
  4.1 0.7 %copy-done.4 = f32[8,2]{0,1:T(2,128)S(1)} copy-done((f32[8,2]{0,1:T(2,128)S(1)}, f32[8,2]{0,1:T(2,128)}, u32[]{:S(2)}) %copy-start.4) | copy-done | bytes 88
  4.8 20.2 %shard_map.76.clean_ref = f32[2,32,8,128]{3,2,1,0:T(8,128)S(1)} custom-call(bf16[263,2,2,2048]{3,2,1,0:T(2,128)(2,1)S(1)} %bitcast.4, bf16[2,2,64,2048]{3,2,1,0:T(8,128)(2,1)S(1)} %bitcast.5, f32[2,8]{1,0:T(2,128)S(1)} %bitcast.6), custom_call_target="tpu_custom_call" | custom-call | tf_op jit(solution)/shard_map/pallas_call | solution.py:337
  25.0 0.0 copy-done.5
  25.0 0.0 copy-done.2
  25.0 9.2 %shard_map.77 = (f32[8,64,256]{2,1,0:T(8,128)}, f32[8,8,64]{2,1,0:T(8,128)}, f32[8,128]{1,0:T(8,128)S(1)}) custom-call(f32[2,32,8,128]{3,2,1,0:T(8,128)S(1)} %shard_map.76.clean_ref, s32[5,2,128]{2,1,0:T(2,128)S(1)} %copy-done.2, s32[8]{0:T(128)S(1)} %copy-done.5), custom_call_target="tpu_custom_call" | custom-call | tf_op jit(solution)/shard_map/pallas_call | solution.py:356
  34.2 0.0 copy-start.3
  34.2 0.6 %copy-done.3 = f32[8,128]{1,0:T(8,128)} copy-done((f32[8,128]{1,0:T(8,128)}, f32[8,128]{1,0:T(8,128)S(1)}, u32[]{:S(2)}) %copy-start.3) | copy-done | bytes 4120
  34.8 8.0 %shard_map.78 = f32[1,64]{1,0:T(1,128)} custom-call(f32[8,128]{1,0:T(8,128)} %copy-done.3), custom_call_target="tpu_custom_call" | custom-call | tf_op jit(solution)/shard_map/pallas_call | solution.py:372
  42.8 1.1 %copy.9 = f32[64]{0:T(128)} copy(f32[64]{0:T(128)} %bitcast.7) | data formatting | bytes 512
Async XLA Ops:
  0.6 24.4 %copy-start.5 = (s32[8]{0:T(128)S(1)}, s32[8]{0:T(128)}, u32[]{:S(2)}) copy-start(s32[8]{0:T(128)} %box_ref.1) | copy-start | bytes 100
  0.6 24.4 %copy-start.2 = (s32[5,2,128]{2,1,0:T(2,128)S(1)}, s32[5,2,128]{2,1,0:T(2,128)}, u32[]{:S(2)}) copy-start(s32[5,2,128]{2,1,0:T(2,128)} %offs_ref.1) | copy-start | bytes 15364
  0.7 2.2 %copy-start = (bf16[1,263,2,2,2048]{4,3,2,1,0:T(2,128)(2,1)S(1)}, bf16[1,263,2,2,2048]{4,3,2,1,0:T(2,128)(2,1)}, u32[]{:S(2)}) copy-start(bf16[1,263,2,2,2048]{4,3,2,1,0:T(2,128)(2,1)} %param.5) | copy-start | bytes 12926980
  2.9 1.2 %copy-start.1 = (bf16[2,2,2048,64]{2,3,1,0:T(8,128)(2,1)S(1)}, bf16[2,2,2048,64]{2,3,1,0:T(8,128)(2,1)}, u32[]{:S(2)}) copy-start(bf16[2,2,2048,64]{2,3,1,0:T(8,128)(2,1)} %param.7) | copy-start | bytes 3145732
  4.1 0.7 %copy-start.4 = (f32[8,2]{0,1:T(2,128)S(1)}, f32[8,2]{0,1:T(2,128)}, u32[]{:S(2)}) copy-start(f32[8,2]{0,1:T(2,128)} %param.6) | copy-start | bytes 196
  34.2 0.6 %copy-start.3 = (f32[8,128]{1,0:T(8,128)}, f32[8,128]{1,0:T(8,128)S(1)}, u32[]{:S(2)}) copy-start(f32[8,128]{1,0:T(8,128)S(1)} %get-tuple-element.8.best_ref) | copy-start | bytes 12292

commit v3 on v2

--- a/solution.py
+++ b/solution.py
@@ -12,7 +12,8 @@
 LANES = 128
 SHORT = 64
 CHUNK = 512
-GRANT = 48 * 1024 * 1024
+GRANT = 58 * 1024 * 1024
+UNROLL = 32
 
 
 def unrolled(count, body):
@@ -45,32 +46,38 @@
     return result
 
 
-def targets(me, devices):
-    return lambda step: lax.rem(me + step, devices)
-
-
-def greet_all(target, devices):
-    barrier = pltpu.get_barrier_semaphore()
-
-    def greet(step, carry):
-        pl.semaphore_signal(barrier, 1, device_id={"freq": target(step)}, device_id_type=MESH)
+def each_other(devices, body):
+    me = lax.axis_index("freq")
+    parts = devices // 2
+    near = me // parts * parts
+    far = parts - near
+
+    def far_step(step, carry):
+        part = lax.rem(me + step, parts)
+        body(step, far + part, part)
         return carry
 
-    lax.fori_loop(1, devices, greet, 0)
-    return barrier
-
-
-def each_other(devices, body):
-    def step_body(step, carry):
-        body(step)
+    def near_step(step, carry):
+        part = lax.rem(me + step, parts)
+        body(parts + step, near + part, part)
         return carry
 
-    lax.fori_loop(1, devices, step_body, 0)
-
-
-def channel_kernel(
-    vol_ref, steer_ref, taps_ref, clean_ref,
-    tiles, wide, total, outgoing, incoming, tile_sems, send_sems, recv_sems,
+    if devices <= UNROLL:
+        for step in range(parts):
+            far_step(step, 0)
+        for step in range(1, parts):
+            near_step(step, 0)
+    else:
+        lax.fori_loop(0, parts, far_step, 0)
+        lax.fori_loop(1, parts, near_step, 0)
+
+
+def kernel(
+    vol_ref, steer_hbm, taps_hbm, offs_hbm, box_hbm,
+    ded_hbm, score_hbm, peak_ref,
+    ded_ref, score_ref, steer_ref, taps_ref, offs_ref, box_ref, tiles, wide, windows, total, outgoing, incoming,
+    clean_ref, plane_a, plane_b, final, best_out, best_in,
+    small_sems, tile_sems, send_sems, recv_sems, best_send, best_recv,
 ):
     devices = lax.axis_size("freq")
     me = lax.axis_index("freq")
@@ -84,8 +91,22 @@
     columns = antennas // LANES
     padded = tiles.shape[1]
     reach = 2 * (SHORT + padded - samples)
-    target = targets(me, devices)
-    barrier = greet_all(target, devices)
+    levels, _, delays = offs_ref.shape
+    rate = delays // channels
+    half = delays // 2
+    small = [
+        pltpu.make_async_copy(source, place, small_sems.at[index])
+        for index, (source, place) in enumerate(
+            (
+                (taps_hbm, taps_ref),
+                (steer_hbm, steer_ref),
+                (offs_hbm, offs_ref),
+                (box_hbm, box_ref),
+            )
+        )
+    ]
+    small[0].start()
+    small[1].start()
 
     def tile_copy(index):
         return pltpu.make_async_copy(
@@ -100,11 +121,24 @@
     for index in range(branches * columns):
         flat(index)[2 * samples :, :] = jnp.zeros((2 * padded - 2 * samples, LANES), jnp.bfloat16)
         tile_copy(index).start()
+    small[2].start()
+    small[3].start()
+
+    barrier = pltpu.get_barrier_semaphore()
+
+    def greet(step, other, part):
+        pl.semaphore_signal(barrier, 1, device_id={"freq": other}, device_id_type=MESH)
+
+    each_other(devices, greet)
+
+    small[1].wait()
 
     for channel in range(2):
         wide[channel] = jnp.transpose(
             jnp.concatenate([steer_ref[channel, 0], steer_ref[channel, 1]], 0)
         )
+
+    small[0].wait()
 
     row = lax.broadcasted_iota(jnp.int32, (SHORT, reach), 0)
     column = lax.broadcasted_iota(jnp.int32, (SHORT, reach), 1)
@@ -119,10 +153,9 @@
             pieces += [high, (band - high.astype(jnp.float32)).astype(jnp.bfloat16)]
         bands.append(jnp.concatenate(pieces, 0))
 
-    def copy_block(block, step, source):
-        other = target(step)
+    def copy_block(block, step, source, other, part):
         return pltpu.make_async_remote_copy(
-            src_ref=outgoing.at[block, lax.rem(other, parts)],
+            src_ref=outgoing.at[block, part],
             dst_ref=incoming.at[block, source],
             send_sem=send_sems.at[block, step],
             recv_sem=recv_sems.at[block, source],
@@ -184,13 +217,29 @@
                 outgoing[block, index, channel] = power[index * per : (index + 1) * per]
         if block == 0:
             pl.semaphore_wait(barrier, devices - 1)
-        each_other(devices, lambda step, block=block: copy_block(block, step, me).start())
+
+        def send(step, other, part, block=block):
+            copy_block(block, step, me, other, part).start()
+
+        each_other(devices, send)
         incoming[block, me] = outgoing[block, lax.rem(me, parts)]
 
+    small[2].wait()
+    small[3].wait()
+    behind = lax.broadcasted_iota(jnp.int32, (samples, samples), 0) - lax.broadcasted_iota(
+        jnp.int32, (samples, samples), 1
+    )
+    for index in range(box_ref.shape[0]):
+        windows[index] = jnp.where(
+            (behind >= 0) & (behind < box_ref[index]), 1.0, 0.0
+        ).astype(jnp.bfloat16)
+
     for block in range(blocks):
-        each_other(
-            devices, lambda step, block=block: copy_block(block, step, target(step)).wait_recv()
-        )
+
+        def receive(step, other, part, block=block):
+            copy_block(block, step, other, other, part).wait_recv()
+
+        each_other(devices, receive)
 
     power = [incoming[t].reshape(channels, per, LANES) for t in range(blocks)]
     level = sum(jnp.sum(tile, axis=-1, keepdims=True) for tile in power) / samples
@@ -201,24 +250,6 @@
         tile = power[t] * inverse
         clean_ref[t] = tile - jnp.sum(tile, axis=0, keepdims=True) / channels
 
-    def drain(step):
-        for block in range(blocks):
-            copy_block(block, step, me).wait_send()
-
-    each_other(devices, drain)
-
-
-def tree_kernel(
-    clean_ref, offs_ref, box_ref, ded_ref, score_ref, best_ref, plane_a, plane_b, final
-):
-    devices = lax.axis_size("freq")
-    me = lax.axis_index("freq")
-    blocks, channels, per, _ = clean_ref.shape
-    parts = devices // 2
-    samples = blocks * LANES
-    levels, _, delays = offs_ref.shape
-    rate = delays // channels
-    half = delays // 2
     lane = lax.broadcasted_iota(jnp.int32, (per, LANES), 1)
 
     def spread_channel(channel):
@@ -265,56 +296,71 @@
             take = pl.ds(index, half, stride=per) if per > 1 else pl.ds(0, half)
             ded_ref[index, :, t * LANES : (t + 1) * LANES] = final[t, take, :]
 
+    ded_copy = pltpu.make_async_copy(ded_ref, ded_hbm, small_sems.at[4])
+    ded_copy.start()
+
     columns = jnp.transpose(ded_ref[...].reshape(per * half, samples))
     high = columns.astype(jnp.bfloat16)
     low = (columns - high.astype(jnp.float32)).astype(jnp.bfloat16)
     pair = jnp.concatenate([high, low], 0)
-    behind = lax.broadcasted_iota(jnp.int32, (samples, samples), 0) - lax.broadcasted_iota(
-        jnp.int32, (samples, samples), 1
-    )
     scores = []
     for index in range(box_ref.shape[0]):
         width = box_ref[index]
-        window = jnp.where((behind >= 0) & (behind < width), 1.0, 0.0).astype(jnp.bfloat16)
+        window = windows[index]
         sums = jnp.dot(
             jnp.concatenate([window, window], 1), pair, preferred_element_type=jnp.float32
         )
         root = jnp.sqrt(jnp.full((1, per * half), width.astype(jnp.float32)))
         scores.append(jnp.max(sums, axis=0, keepdims=True) / root)
     scores = jnp.concatenate(scores, 0)
-    lane = lax.broadcasted_iota(jnp.int32, best_ref.shape, 1)
-    best = jnp.full(best_ref.shape, jnp.finfo(jnp.float32).min, jnp.float32)
+    lane = lax.broadcasted_iota(jnp.int32, best_out.shape, 1)
+    best = jnp.full(best_out.shape, jnp.finfo(jnp.float32).min, jnp.float32)
     for index in range(per):
         mine = scores[:, index * half : (index + 1) * half]
         score_ref[index] = mine
         peak = jnp.max(jnp.max(mine, axis=1, keepdims=True), axis=0, keepdims=True)
         best = jnp.where(lane == lax.rem(me, parts) * per + index, peak, best)
-    best_ref[...] = best
-
-
-def peak_kernel(best_ref, peak_ref, best_in, best_send, best_recv):
-    devices = lax.axis_size("freq")
-    me = lax.axis_index("freq")
-    target = targets(me, devices)
-    barrier = greet_all(target, devices)
-    best_in[me] = best_ref[...]
-    pl.semaphore_wait(barrier, devices - 1)
-
-    def copy_best(step, source):
+    best_out[...] = best
+    best_in[me] = best
+
+    def copy_best(step, source, other):
         return pltpu.make_async_remote_copy(
-            src_ref=best_ref,
+            src_ref=best_out,
             dst_ref=best_in.at[source],
             send_sem=best_send.at[step],
             recv_sem=best_recv.at[source],
-            device_id={"freq": target(step)},
+            device_id={"freq": other},
             device_id_type=MESH,
         )
 
-    each_other(devices, lambda step: copy_best(step, me).start())
-    each_other(devices, lambda step: copy_best(step, target(step)).wait_recv())
+    each_other(devices, lambda step, other, part: copy_best(step, me, other).start())
+
+    score_copy = pltpu.make_async_copy(score_ref, score_hbm, small_sems.at[5])
+    score_copy.start()
+
+    def drain(step, other, part):
+        for block in range(blocks):
+            copy_block(block, step, me, other, part).wait_send()
+
+    each_other(devices, drain)
+    each_other(devices, lambda step, other, part: copy_best(step, other, other).wait_recv())
     peaks = jnp.max(best_in[...], axis=0)
-    peak_ref[...] = peaks[:1, : peak_ref.shape[1]]
-    each_other(devices, lambda step: copy_best(step, me).wait_send())
+    peak_ref[...] = peaks[:1, :beams]
+    each_other(devices, lambda step, other, part: copy_best(step, me, other).wait_send())
+    ded_copy.wait()
+    score_copy.wait()
+
+
+def finish_kernel(ded_ref, score_ref, peak_ref, ded_out, score_out, peak_out, sems):
+    copies = [
+        pltpu.make_async_copy(ded_ref, ded_out, sems.at[0]),
+        pltpu.make_async_copy(score_ref, score_out, sems.at[1]),
+        pltpu.make_async_copy(peak_ref, peak_out, sems.at[2]),
+    ]
+    for copy in copies:
+        copy.start()
+    for copy in copies:
+        copy.wait()
 
 
 def shards(voltages, pfb_taps, steering, fdmt_offsets, box_lengths):
@@ -332,55 +378,62 @@
     padded = samples + -(-(tap_total - 1) // 8) * 8
     tile_total = branches * antennas // LANES
     vmem = pl.BlockSpec(memory_space=pltpu.VMEM)
-    smem = pl.BlockSpec(memory_space=pltpu.SMEM)
     f32 = jnp.float32
-    cleaned = pl.pallas_call(
-        channel_kernel,
-        out_shape=jax.ShapeDtypeStruct((blocks, channels, per, LANES), f32),
-        in_specs=[pl.BlockSpec(memory_space=pl.ANY), vmem, smem],
-        out_specs=vmem,
+    hbm = pl.BlockSpec(memory_space=pltpu.HBM)
+    results = (
+        jax.ShapeDtypeStruct((per, half, samples), f32),
+        jax.ShapeDtypeStruct((per, boxes, half), f32),
+        jax.ShapeDtypeStruct((1, beams), f32),
+    )
+    found = pl.pallas_call(
+        kernel,
+        out_shape=results,
+        in_specs=[hbm] * 5,
+        out_specs=(hbm, hbm, vmem),
         scratch_shapes=[
+            pltpu.VMEM((per, half, samples), f32),
+            pltpu.VMEM((per, boxes, half), f32),
+            pltpu.VMEM((2, 2, beams, antennas), jnp.bfloat16),
+            pltpu.SMEM((branches, tap_total), f32),
+            pltpu.SMEM((levels, 2, delays), jnp.int32),
+            pltpu.SMEM((boxes,), jnp.int32),
             pltpu.VMEM((tile_total, padded, pair, LANES), jnp.bfloat16),
             pltpu.VMEM((2, antennas, 2 * beams), jnp.bfloat16),
+            pltpu.VMEM((boxes, samples, samples), jnp.bfloat16),
             pltpu.VMEM((2, 2 * LANES, 2 * beams), f32),
             pltpu.VMEM((blocks, beams // per, 2, per, LANES), f32),
             pltpu.VMEM((blocks, devices, 2, per, LANES), f32),
+            pltpu.VMEM((blocks, channels, per, LANES), f32),
+            pltpu.VMEM((blocks, delays, per, LANES), f32),
+            pltpu.VMEM((blocks, delays, per, LANES), f32),
+            pltpu.VMEM((blocks, half * per, LANES), f32),
+            pltpu.VMEM((8, LANES), f32),
+            pltpu.VMEM((devices, 8, LANES), f32),
+            pltpu.SemaphoreType.DMA((6,)),
             pltpu.SemaphoreType.DMA((tile_total,)),
             pltpu.SemaphoreType.DMA((blocks, devices)),
             pltpu.SemaphoreType.DMA((blocks, devices)),
+            pltpu.SemaphoreType.DMA((devices,)),
+            pltpu.SemaphoreType.DMA((devices,)),
         ],
         compiler_params=pltpu.CompilerParams(
             collective_id=0, has_side_effects=True, vmem_limit_bytes=GRANT
         ),
-    )(voltages[0], jnp.transpose(steering, (0, 1, 3, 2)), pfb_taps.T)
-    dedispersed, box_scores, best = pl.pallas_call(
-        tree_kernel,
-        out_shape=(
-            jax.ShapeDtypeStruct((per, half, samples), f32),
-            jax.ShapeDtypeStruct((per, boxes, half), f32),
-            jax.ShapeDtypeStruct((8, LANES), f32),
-        ),
-        in_specs=[vmem, smem, smem],
-        out_specs=(vmem, vmem, vmem),
-        scratch_shapes=[
-            pltpu.VMEM((blocks, delays, per, LANES), f32),
-            pltpu.VMEM((blocks, delays, per, LANES), f32),
-            pltpu.VMEM((blocks, half * per, LANES), f32),
-        ],
+    )(
+        voltages[0],
+        jnp.transpose(steering, (0, 1, 3, 2)),
+        pfb_taps.T,
+        fdmt_offsets,
+        box_lengths,
+    )
+    dedispersed, box_scores, peaks = pl.pallas_call(
+        finish_kernel,
+        out_shape=results,
+        in_specs=[hbm] * 3,
+        out_specs=(hbm, hbm, hbm),
+        scratch_shapes=[pltpu.SemaphoreType.DMA((3,))],
         compiler_params=pltpu.CompilerParams(vmem_limit_bytes=GRANT),
-    )(cleaned, fdmt_offsets, box_lengths)
-    peaks = pl.pallas_call(
-        peak_kernel,
-        out_shape=jax.ShapeDtypeStruct((1, beams), f32),
-        in_specs=[vmem],
-        out_specs=vmem,
-        scratch_shapes=[
-            pltpu.VMEM((devices, 8, LANES), f32),
-            pltpu.SemaphoreType.DMA((devices,)),
-            pltpu.SemaphoreType.DMA((devices,)),
-        ],
-        compiler_params=pltpu.CompilerParams(collective_id=1, has_side_effects=True),
-    )(best)
+    )(*found)
     return dedispersed, box_scores, peaks.reshape(beams)
 
 

time: 44.1 us -> 49.5 us (1.12)
  Pallas kernels: 37.4 us -> 48.7 us
  local copies, waits for them, and re-layouts: 5.84 us -> 0 us
    pallas_call x3 -> x2, Pallas kernels: 37.4 us -> 48.7 us  [the longest x1 30.7 us: shards(): pl.pallas_call(kernel, out_shape=results, in_specs=[hbm] * 5, out_specs=(...]
    unnamed x13 -> x0, local copies, waits for them, and re-layouts: 5.84 us -> none
where the time goes in v3:
time: 49.5 us; the launch traced here: 49.3 us
  Pallas kernels  48.7 us (98%)
  between operations  0.64 us (1%)
    pallas_call x1, Pallas kernels, shards(): pl.pallas_call(kernel, out_shape=results, in_specs=[hbm] * 5, out_specs=(...  30.7 us
    pallas_call x1, Pallas kernels, shards(): pl.pallas_call(finish_kernel, out_shape=results, in_specs=[hbm] * 3, out_...  18 us

profile of v3, /device:TPU:0, one launch (start us, length us, event | category | flops | bytes accessed | tf_op | source)
XLA Modules:
  0.0 49.3 jit_solution(18343235099447453320)
XLA Ops:
  0.6 30.7 %shard_map.76 = (f32[8,64,256]{2,1,0:T(8,128)}, f32[8,8,64]{2,1,0:T(8,128)}, f32[1,64]{1,0:T(1,128)}) custom-call(bf16[263,2,2,2048]{3,2,1,0:T(2,128)(2,1)} %bitcast.4, bf16[2,2,64,2048]{3,2,1,0:T(8,128)(2,1)} %bitcast.5, f32[2,8]{1,0:T(2,128)} %bitcast.6, s32[5,2,128]{2,1,0:T(2,128)} %offs_hbm.1, s32[8]{0:T(128)} %box_hbm.1), custom_call_target="tpu_custom_call" | custom-call | tf_op jit(solution)/shard_map/pallas_call | solution.py:388
  31.3 18.0 %shard_map.77 = (f32[8,64,256]{2,1,0:T(8,128)}, f32[8,8,64]{2,1,0:T(8,128)}, f32[1,64]{1,0:T(1,128)}) custom-call(f32[8,64,256]{2,1,0:T(8,128)} %get-tuple-element.9.ded_ref, f32[8,8,64]{2,1,0:T(8,128)} %get-tuple-element.10.score_ref, f32[1,64]{1,0:T(1,128)} %get-tuple-element.11.peak_ref), custom_call_target="tpu_custom_call" | custom-call | tf_op jit(solution)/shard_map/pallas_call | solution.py:429

commit v4 on v3

--- a/solution.py
+++ b/solution.py
@@ -10,7 +10,7 @@
 
 MESH = pl.DeviceIdType.MESH
 LANES = 128
-SHORT = 64
+SHORTS = (48, 48, 32)
 CHUNK = 512
 GRANT = 58 * 1024 * 1024
 UNROLL = 32
@@ -90,7 +90,7 @@
     channels = 2 * devices
     columns = antennas // LANES
     padded = tiles.shape[1]
-    reach = 2 * (SHORT + padded - samples)
+    ahead = padded - samples
     levels, _, delays = offs_ref.shape
     rate = delays // channels
     half = delays // 2
@@ -108,11 +108,15 @@
     small[0].start()
     small[1].start()
 
-    def tile_copy(index):
+    def tile_copy(block, index):
+        begin = block * LANES + ahead if block else 0
+        size = min((block + 1) * LANES + ahead, inputs) - begin
         return pltpu.make_async_copy(
-            vol_ref.at[:, index % branches, :, pl.ds(index // branches * LANES, LANES)],
-            tiles.at[index, pl.ds(0, inputs)],
-            tile_sems.at[index],
+            vol_ref.at[
+                pl.ds(begin, size), index % branches, :, pl.ds(index // branches * LANES, LANES)
+            ],
+            tiles.at[index, pl.ds(begin, size)],
+            tile_sems.at[block, index],
         )
 
     def flat(index):
@@ -120,7 +124,9 @@
 
     for index in range(branches * columns):
         flat(index)[2 * samples :, :] = jnp.zeros((2 * padded - 2 * samples, LANES), jnp.bfloat16)
-        tile_copy(index).start()
+    for block in range(blocks):
+        for index in range(branches * columns):
+            tile_copy(block, index).start()
     small[2].start()
     small[3].start()
 
@@ -140,18 +146,22 @@
 
     small[0].wait()
 
-    row = lax.broadcasted_iota(jnp.int32, (SHORT, reach), 0)
-    column = lax.broadcasted_iota(jnp.int32, (SHORT, reach), 1)
-    bands = []
-    for branch in range(branches):
-        pieces = []
-        for part in range(2):
-            band = jnp.zeros((SHORT, reach), jnp.float32)
-            for tap in range(tap_total):
-                band = jnp.where(column == 2 * (row + tap) + part, taps_ref[branch, tap], band)
-            high = band.astype(jnp.bfloat16)
-            pieces += [high, (band - high.astype(jnp.float32)).astype(jnp.bfloat16)]
-        bands.append(jnp.concatenate(pieces, 0))
+    bands = {}
+    for size in set(SHORTS):
+        reach = 2 * (size + ahead)
+        row = lax.broadcasted_iota(jnp.int32, (size, 2 * reach), 0)
+        column = lax.broadcasted_iota(jnp.int32, (size, 2 * reach), 1)
+        first_copy = column < reach
+        column = jnp.where(first_copy, column, column - reach)
+        for branch in range(branches):
+            pieces = []
+            for part in range(2):
+                band = jnp.zeros((size, 2 * reach), jnp.float32)
+                for tap in range(tap_total):
+                    band = jnp.where(column == 2 * (row + tap) + part, taps_ref[branch, tap], band)
+                high = band.astype(jnp.bfloat16).astype(jnp.float32)
+                pieces.append(jnp.where(first_copy, high, band - high).astype(jnp.bfloat16))
+            bands[size, branch] = jnp.concatenate(pieces, 0)
 
     def copy_block(block, step, source, other, part):
         return pltpu.make_async_remote_copy(
@@ -170,12 +180,13 @@
     for block in range(blocks):
         for start in range(0, antennas, CHUNK):
             first = start // LANES
-            if block == 0:
-                for index in range(first * branches, (first + CHUNK // LANES) * branches):
-                    tile_copy(index).wait()
+            for index in range(first * branches, (first + CHUNK // LANES) * branches):
+                tile_copy(block, index).wait()
             fine = [[[], []], [[], []]]
-            for short in range(0, LANES, SHORT):
-                rows = pl.ds(2 * (block * LANES + short), reach)
+            short = block * LANES
+            for size in SHORTS:
+                rows = pl.ds(2 * short, 2 * (size + ahead))
+                short += size
                 filtered = []
                 for branch in range(branches):
                     volume = jnp.concatenate(
@@ -185,14 +196,12 @@
                         ],
                         1,
                     )
-                    both = jnp.dot(bands[branch], volume, preferred_element_type=jnp.float32)
-                    filtered.append(
-                        [
-                            both[2 * part * SHORT : (2 * part + 1) * SHORT]
-                            + both[(2 * part + 1) * SHORT : (2 * part + 2) * SHORT]
-                            for part in range(2)
-                        ]
+                    both = jnp.dot(
+                        bands[size, branch],
+                        jnp.concatenate([volume, volume], 0),
+                        preferred_element_type=jnp.float32,
                     )
+                    filtered.append([both[:size], both[size:]])
                 for part in range(2):
                     even, odd = filtered[0][part], filtered[1][part]
                     fine[0][part].append((even + odd).astype(jnp.bfloat16))
@@ -351,16 +360,10 @@
     score_copy.wait()
 
 
-def finish_kernel(ded_ref, score_ref, peak_ref, ded_out, score_out, peak_out, sems):
-    copies = [
-        pltpu.make_async_copy(ded_ref, ded_out, sems.at[0]),
-        pltpu.make_async_copy(score_ref, score_out, sems.at[1]),
-        pltpu.make_async_copy(peak_ref, peak_out, sems.at[2]),
-    ]
-    for copy in copies:
-        copy.start()
-    for copy in copies:
-        copy.wait()
+def finish_kernel(ded_ref, score_ref, peak_ref, ded_out, score_out, peak_out):
+    ded_out[...] = ded_ref[...]
+    score_out[...] = score_ref[...]
+    peak_out[...] = peak_ref[...]
 
 
 def shards(voltages, pfb_taps, steering, fdmt_offsets, box_lengths):
@@ -410,7 +413,7 @@
             pltpu.VMEM((8, LANES), f32),
             pltpu.VMEM((devices, 8, LANES), f32),
             pltpu.SemaphoreType.DMA((6,)),
-            pltpu.SemaphoreType.DMA((tile_total,)),
+            pltpu.SemaphoreType.DMA((blocks, tile_total)),
             pltpu.SemaphoreType.DMA((blocks, devices)),
             pltpu.SemaphoreType.DMA((blocks, devices)),
             pltpu.SemaphoreType.DMA((devices,)),
@@ -429,9 +432,8 @@
     dedispersed, box_scores, peaks = pl.pallas_call(
         finish_kernel,
         out_shape=results,
-        in_specs=[hbm] * 3,
-        out_specs=(hbm, hbm, hbm),
-        scratch_shapes=[pltpu.SemaphoreType.DMA((3,))],
+        in_specs=[vmem] * 3,
+        out_specs=(vmem, vmem, vmem),
         compiler_params=pltpu.CompilerParams(vmem_limit_bytes=GRANT),
     )(*found)
     return dedispersed, box_scores, peaks.reshape(beams)

time: 49.5 us -> 34.5 us (0.70)
  Pallas kernels: 48.7 us -> 33.7 us
    pallas_call x1, Pallas kernels: 18 us -> 1.9 us  [shards(): pl.pallas_call(finish_kernel, out_shape=results, in_specs=[vmem] * 3, out...]
    pallas_call x1, Pallas kernels: 30.7 us -> 31.8 us  [shards(): pl.pallas_call(kernel, out_shape=results, in_specs=[hbm] * 5, out_specs=(...]
where the time goes in v4:
time: 34.5 us; the launch traced here: 34.3 us
  Pallas kernels  33.7 us (98%)
  between operations  0.64 us (2%)
    pallas_call x1, Pallas kernels, shards(): pl.pallas_call(kernel, out_shape=results, in_specs=[hbm] * 5, out_specs=(...  31.8 us
    pallas_call x1, Pallas kernels, shards(): pl.pallas_call(finish_kernel, out_shape=results, in_specs=[vmem] * 3, out...  1.9 us

profile of v4, /device:TPU:0, one launch (start us, length us, event | category | flops | bytes accessed | tf_op | source)
XLA Modules:
  0.0 34.3 jit_solution(6434297866129596711)
XLA Ops:
  0.6 31.8 %shard_map.76 = (f32[8,64,256]{2,1,0:T(8,128)}, f32[8,8,64]{2,1,0:T(8,128)}, f32[1,64]{1,0:T(1,128)}) custom-call(bf16[263,2,2,2048]{3,2,1,0:T(2,128)(2,1)} %bitcast.4, bf16[2,2,64,2048]{3,2,1,0:T(8,128)(2,1)} %bitcast.5, f32[2,8]{1,0:T(2,128)} %bitcast.6, s32[5,2,128]{2,1,0:T(2,128)} %offs_hbm.1, s32[8]{0:T(128)} %box_hbm.1), custom_call_target="tpu_custom_call" | custom-call | tf_op jit(solution)/shard_map/pallas_call | solution.py:391
  32.4 1.9 %shard_map.77 = (f32[8,64,256]{2,1,0:T(8,128)}, f32[8,8,64]{2,1,0:T(8,128)}, f32[1,64]{1,0:T(1,128)}) custom-call(f32[8,64,256]{2,1,0:T(8,128)} %get-tuple-element.9.ded_ref, f32[8,8,64]{2,1,0:T(8,128)} %get-tuple-element.10.score_ref, f32[1,64]{1,0:T(1,128)} %get-tuple-element.11.peak_ref), custom_call_target="tpu_custom_call" | custom-call | tf_op jit(solution)/shard_map/pallas_call | solution.py:432

commit v5 on v4

--- a/solution.py
+++ b/solution.py
@@ -77,7 +77,7 @@
     ded_hbm, score_hbm, peak_ref,
     ded_ref, score_ref, steer_ref, taps_ref, offs_ref, box_ref, tiles, wide, windows, total, outgoing, incoming,
     clean_ref, plane_a, plane_b, final, best_out, best_in,
-    small_sems, tile_sems, send_sems, recv_sems, best_send, best_recv,
+    small_sems, tile_sems, send_sems, recv_sems,
 ):
     devices = lax.axis_size("freq")
     me = lax.axis_index("freq")
@@ -108,15 +108,13 @@
     small[0].start()
     small[1].start()
 
-    def tile_copy(block, index):
-        begin = block * LANES + ahead if block else 0
-        size = min((block + 1) * LANES + ahead, inputs) - begin
+    group = CHUNK // LANES * branches
+
+    def tile_copy(index):
         return pltpu.make_async_copy(
-            vol_ref.at[
-                pl.ds(begin, size), index % branches, :, pl.ds(index // branches * LANES, LANES)
-            ],
-            tiles.at[index, pl.ds(begin, size)],
-            tile_sems.at[block, index],
+            vol_ref.at[:, index % branches, :, pl.ds(index // branches * LANES, LANES)],
+            tiles.at[index, pl.ds(0, inputs)],
+            tile_sems.at[index // group],
         )
 
     def flat(index):
@@ -124,9 +122,8 @@
 
     for index in range(branches * columns):
         flat(index)[2 * samples :, :] = jnp.zeros((2 * padded - 2 * samples, LANES), jnp.bfloat16)
-    for block in range(blocks):
-        for index in range(branches * columns):
-            tile_copy(block, index).start()
+    for index in range(branches * columns):
+        tile_copy(index).start()
     small[2].start()
     small[3].start()
 
@@ -163,12 +160,23 @@
                 pieces.append(jnp.where(first_copy, high, band - high).astype(jnp.bfloat16))
             bands[size, branch] = jnp.concatenate(pieces, 0)
 
-    def copy_block(block, step, source, other, part):
+    def every(block, place):
+        whole = place.at[pl.ds(0, devices - 1)]
+        return pltpu.make_async_remote_copy(
+            src_ref=whole,
+            dst_ref=whole,
+            send_sem=send_sems.at[block],
+            recv_sem=recv_sems.at[block],
+            device_id={"freq": lax.rem(me + 1, devices)},
+            device_id_type=MESH,
+        )
+
+    def copy_block(block, source, other, part):
         return pltpu.make_async_remote_copy(
             src_ref=outgoing.at[block, part],
             dst_ref=incoming.at[block, source],
-            send_sem=send_sems.at[block, step],
-            recv_sem=recv_sems.at[block, source],
+            send_sem=send_sems.at[block],
+            recv_sem=recv_sems.at[block],
             device_id={"freq": other},
             device_id_type=MESH,
         )
@@ -180,8 +188,9 @@
     for block in range(blocks):
         for start in range(0, antennas, CHUNK):
             first = start // LANES
-            for index in range(first * branches, (first + CHUNK // LANES) * branches):
-                tile_copy(block, index).wait()
+            if block == 0:
+                arrived = tiles.at[pl.ds(first * branches, group), pl.ds(0, inputs)]
+                pltpu.make_async_copy(arrived, arrived, tile_sems.at[start // CHUNK]).wait()
             fine = [[[], []], [[], []]]
             short = block * LANES
             for size in SHORTS:
@@ -228,7 +237,7 @@
             pl.semaphore_wait(barrier, devices - 1)
 
         def send(step, other, part, block=block):
-            copy_block(block, step, me, other, part).start()
+            copy_block(block, me, other, part).start()
 
         each_other(devices, send)
         incoming[block, me] = outgoing[block, lax.rem(me, parts)]
@@ -244,11 +253,7 @@
         ).astype(jnp.bfloat16)
 
     for block in range(blocks):
-
-        def receive(step, other, part, block=block):
-            copy_block(block, step, other, other, part).wait_recv()
-
-        each_other(devices, receive)
+        every(block, incoming.at[block]).wait_recv()
 
     power = [incoming[t].reshape(channels, per, LANES) for t in range(blocks)]
     level = sum(jnp.sum(tile, axis=-1, keepdims=True) for tile in power) / samples
@@ -332,30 +337,25 @@
     best_out[...] = best
     best_in[me] = best
 
-    def copy_best(step, source, other):
-        return pltpu.make_async_remote_copy(
+    def send_best(step, other, part):
+        pltpu.make_async_remote_copy(
             src_ref=best_out,
-            dst_ref=best_in.at[source],
-            send_sem=best_send.at[step],
-            recv_sem=best_recv.at[source],
+            dst_ref=best_in.at[me],
+            send_sem=send_sems.at[blocks],
+            recv_sem=recv_sems.at[blocks],
             device_id={"freq": other},
             device_id_type=MESH,
-        )
-
-    each_other(devices, lambda step, other, part: copy_best(step, me, other).start())
-
+        ).start()
+
+    each_other(devices, send_best)
     score_copy = pltpu.make_async_copy(score_ref, score_hbm, small_sems.at[5])
     score_copy.start()
-
-    def drain(step, other, part):
-        for block in range(blocks):
-            copy_block(block, step, me, other, part).wait_send()
-
-    each_other(devices, drain)
-    each_other(devices, lambda step, other, part: copy_best(step, other, other).wait_recv())
+    every(blocks, best_in).wait_recv()
     peaks = jnp.max(best_in[...], axis=0)
     peak_ref[...] = peaks[:1, :beams]
-    each_other(devices, lambda step, other, part: copy_best(step, me, other).wait_send())
+    for block in range(blocks):
+        every(block, incoming.at[block]).wait_send()
+    every(blocks, best_in).wait_send()
     ded_copy.wait()
     score_copy.wait()
 
@@ -413,11 +413,9 @@
             pltpu.VMEM((8, LANES), f32),
             pltpu.VMEM((devices, 8, LANES), f32),
             pltpu.SemaphoreType.DMA((6,)),
-            pltpu.SemaphoreType.DMA((blocks, tile_total)),
-            pltpu.SemaphoreType.DMA((blocks, devices)),
-            pltpu.SemaphoreType.DMA((blocks, devices)),
-            pltpu.SemaphoreType.DMA((devices,)),
-            pltpu.SemaphoreType.DMA((devices,)),
+            pltpu.SemaphoreType.DMA((antennas // CHUNK,)),
+            pltpu.SemaphoreType.DMA((blocks + 1,)),
+            pltpu.SemaphoreType.DMA((blocks + 1,)),
         ],
         compiler_params=pltpu.CompilerParams(
             collective_id=0, has_side_effects=True, vmem_limit_bytes=GRANT

time: 34.5 us -> 32.5 us (0.942)
  Pallas kernels: 33.7 us -> 31.7 us
    pallas_call x1, Pallas kernels: 31.8 us -> 29.8 us  [shards(): pl.pallas_call(kernel, out_shape=results, in_specs=[hbm] * 5, out_specs=(...]
where the time goes in v5:
time: 32.5 us; the launch traced here: 32.3 us
  Pallas kernels  31.7 us (98%)
  between operations  0.64 us (2%)
    pallas_call x1, Pallas kernels, shards(): pl.pallas_call(kernel, out_shape=results, in_specs=[hbm] * 5, out_specs=(...  29.8 us
    pallas_call x1, Pallas kernels, shards(): pl.pallas_call(finish_kernel, out_shape=results, in_specs=[vmem] * 3, out...  1.9 us

profile of v5, /device:TPU:0, one launch (start us, length us, event | category | flops | bytes accessed | tf_op | source)
XLA Modules:
  0.0 32.3 jit_solution(4261903207299265880)
XLA Ops:
  0.6 29.8 %shard_map.76 = (f32[8,64,256]{2,1,0:T(8,128)}, f32[8,8,64]{2,1,0:T(8,128)}, f32[1,64]{1,0:T(1,128)}) custom-call(bf16[263,2,2,2048]{3,2,1,0:T(2,128)(2,1)} %bitcast.4, bf16[2,2,64,2048]{3,2,1,0:T(8,128)(2,1)} %bitcast.5, f32[2,8]{1,0:T(2,128)} %bitcast.6, s32[5,2,128]{2,1,0:T(2,128)} %offs_hbm.1, s32[8]{0:T(128)} %box_hbm.1), custom_call_target="tpu_custom_call" | custom-call | tf_op jit(solution)/shard_map/pallas_call | solution.py:391
  30.4 1.9 %shard_map.77 = (f32[8,64,256]{2,1,0:T(8,128)}, f32[8,8,64]{2,1,0:T(8,128)}, f32[1,64]{1,0:T(1,128)}) custom-call(f32[8,64,256]{2,1,0:T(8,128)} %get-tuple-element.9.ded_ref, f32[8,8,64]{2,1,0:T(8,128)} %get-tuple-element.10.score_ref, f32[1,64]{1,0:T(1,128)} %get-tuple-element.11.peak_ref), custom_call_target="tpu_custom_call" | custom-call | tf_op jit(solution)/shard_map/pallas_call | solution.py:430

commit v6 on v5

--- a/solution.py
+++ b/solution.py
@@ -137,9 +137,8 @@
     small[1].wait()
 
     for channel in range(2):
-        wide[channel] = jnp.transpose(
-            jnp.concatenate([steer_ref[channel, 0], steer_ref[channel, 1]], 0)
-        )
+        wide[channel, :beams] = steer_ref[channel, 0]
+        wide[channel, beams:] = steer_ref[channel, 1]
 
     small[0].wait()
 
@@ -216,9 +215,10 @@
                     fine[0][part].append((even + odd).astype(jnp.bfloat16))
                     fine[1][part].append((even - odd).astype(jnp.bfloat16))
             for channel in range(2):
-                product = jnp.dot(
+                product = lax.dot_general(
                     jnp.concatenate(fine[channel][0] + fine[channel][1], 0),
-                    wide[channel, pl.ds(start, CHUNK), :],
+                    wide[channel, :, pl.ds(start, CHUNK)],
+                    (((1,), (1,)), ((), ())),
                     preferred_element_type=jnp.float32,
                 )
                 if start:
@@ -401,7 +401,7 @@
             pltpu.SMEM((levels, 2, delays), jnp.int32),
             pltpu.SMEM((boxes,), jnp.int32),
             pltpu.VMEM((tile_total, padded, pair, LANES), jnp.bfloat16),
-            pltpu.VMEM((2, antennas, 2 * beams), jnp.bfloat16),
+            pltpu.VMEM((2, 2 * beams, antennas), jnp.bfloat16),
             pltpu.VMEM((boxes, samples, samples), jnp.bfloat16),
             pltpu.VMEM((2, 2 * LANES, 2 * beams), f32),
             pltpu.VMEM((blocks, beams // per, 2, per, LANES), f32),

time: 32.5 us -> 32.1 us (0.988)
  Pallas kernels: 31.7 us -> 31.3 us
    pallas_call x1, Pallas kernels: 29.8 us -> 29.4 us  [shards(): pl.pallas_call(kernel, out_shape=results, in_specs=[hbm] * 5, out_specs=(...]
where the time goes in v6:
time: 32.1 us; the launch traced here: 32 us
  Pallas kernels  31.3 us (98%)
  between operations  0.64 us (2%)
    pallas_call x1, Pallas kernels, shards(): pl.pallas_call(kernel, out_shape=results, in_specs=[hbm] * 5, out_specs=(...  29.4 us
    pallas_call x1, Pallas kernels, shards(): pl.pallas_call(finish_kernel, out_shape=results, in_specs=[vmem] * 3, out...  1.9 us

profile of v6, /device:TPU:0, one launch (start us, length us, event | category | flops | bytes accessed | tf_op | source)
XLA Modules:
  0.0 32.0 jit_solution(2546997972697315776)
XLA Ops:
  0.6 29.4 %shard_map.76 = (f32[8,64,256]{2,1,0:T(8,128)}, f32[8,8,64]{2,1,0:T(8,128)}, f32[1,64]{1,0:T(1,128)}) custom-call(bf16[263,2,2,2048]{3,2,1,0:T(2,128)(2,1)} %bitcast.4, bf16[2,2,64,2048]{3,2,1,0:T(8,128)(2,1)} %bitcast.5, f32[2,8]{1,0:T(2,128)} %bitcast.6, s32[5,2,128]{2,1,0:T(2,128)} %offs_hbm.1, s32[8]{0:T(128)} %box_hbm.1), custom_call_target="tpu_custom_call" | custom-call | tf_op jit(solution)/shard_map/pallas_call | solution.py:391
  30.1 1.9 %shard_map.77 = (f32[8,64,256]{2,1,0:T(8,128)}, f32[8,8,64]{2,1,0:T(8,128)}, f32[1,64]{1,0:T(1,128)}) custom-call(f32[8,64,256]{2,1,0:T(8,128)} %get-tuple-element.9.ded_ref, f32[8,8,64]{2,1,0:T(8,128)} %get-tuple-element.10.score_ref, f32[1,64]{1,0:T(1,128)} %get-tuple-element.11.peak_ref), custom_call_target="tpu_custom_call" | custom-call | tf_op jit(solution)/shard_map/pallas_call | solution.py:430
